TPU v7x, 32 devices: a whole 2x2x4 slice. The times are simulated.
32 devices in a mesh: ctx: 8 (over z, y), et: 4 (over x, core).
Axes of the slice: x: 2, y: 2, z: 4, core: 2. Of those that a mesh axis runs over, the one named last changes fastest.
Arguments:
- hidden_in: float32 [1024, 4096], P('ctx', 'et'), may hold values from -60 to 60
- queries: bfloat16 [1024, 4096], P('ctx', 'et'), may hold values from -120 to 120
- keys: bfloat16 [1024, 256], P('ctx'), may hold values from -4.5 to 4.5
- values: bfloat16 [1024, 256], P('ctx'), may hold values from -4 to 4
- out_proj: bfloat16 [4096, 4096], P(None, 'et'), may hold values from -0.5 to 0.5
- norm_gain: float32 [4096], P('et'), may hold values from 0.2 to 2
- expert_ids: int32 [1024, 8], P('ctx'), may hold values from 0 to 127, all different within a row; in each aligned block of 128 rows (0 to 127, 128 to 255, ...) at most 12 rows name the same one
- route_weights: float32 [1024, 8], P('ctx'), may hold values from 0.05 to 1
- w_gate: bfloat16 [8, 4096, 1536], P('ctx', None, 'et'), may hold values from -0.09375 to 0.09375
- w_up: bfloat16 [8, 4096, 1536], P('ctx', None, 'et'), may hold values from -0.09375 to 0.09375
- w_down: bfloat16 [8, 1536, 4096], P('ctx', 'et'), may hold values from -0.15625 to 0.15625
Outputs:
- layer_out: float32 [1024, 4096], P('ctx', 'et')
Inputs may be any that keep to these rules, and one draw needn't show every extreme that they name: `expert_ids`: each row names 8 different experts; within the 128 rows of one device no expert is named by more than 12 rows.
All inputs are finite; a program needn't handle non-finite values.
Results may differ from a plain program's by a relative error of at most 0.0025.
Values may be sent and summed in bfloat16 or wider, within the bound.
A program may use at most 64 MiB of HBM per device.

v0:
```python
import math

import jax
import jax.numpy as jnp
from jax import lax
from jax.sharding import PartitionSpec as P

D = 4096
HEADS = 32
KV_HEADS = 2
HD = 128
CAP = 12


epsilon = 1e-06
masked_score = -1e30


def body(
    hidden_in,
    queries,
    keys,
    values,
    out_proj,
    norm_gain,
    expert_ids,
    route_weights,
    w_gate,
    w_up,
    w_down,
):
    experts_here = lax.axis_size("ctx")
    tok_rows = hidden_in.shape[0]
    local_heads = queries.shape[1] // HD
    head_group = HEADS // KV_HEADS
    score_scale = 1.0 / math.sqrt(HD)
    kv_index = lax.axis_index("et") * local_heads // head_group
    key_local = lax.dynamic_slice_in_dim(keys, kv_index * HD, HD, 1)
    value_local = lax.dynamic_slice_in_dim(values, kv_index * HD, HD, 1)
    query_heads = queries.reshape(tok_rows, local_heads, HD)
    query_pos = lax.axis_index("ctx") * tok_rows + jnp.arange(tok_rows, dtype=jnp.int32)
    run_max = jnp.full((local_heads, tok_rows), masked_score, jnp.float32)
    key_piece = lax.all_gather(key_local, "ctx", axis=0, tiled=True)
    value_piece = lax.all_gather(value_local, "ctx", axis=0, tiled=True)
    key_count = key_piece.shape[0]
    scores = (
        jnp.einsum("thd,kd->htk", query_heads, key_piece, preferred_element_type=jnp.float32)
        * score_scale
    )
    key_pos = jnp.arange(key_count, dtype=jnp.int32)
    allowed = key_pos[None, None, :] <= query_pos[None, :, None]
    scores = jnp.where(allowed, scores, masked_score)
    new_max = jnp.maximum(run_max, jnp.max(scores, axis=2))
    probs = jnp.where(allowed, jnp.exp(scores - new_max[:, :, None]), 0.0)
    new_sum = jnp.sum(probs, axis=2)
    update = jnp.einsum(
        "htk,kd->htd", probs.astype(jnp.bfloat16), value_piece, preferred_element_type=jnp.float32
    )
    attn = (
        jnp.transpose(update / new_sum[:, :, None], (1, 0, 2))
        .reshape(tok_rows, local_heads * HD)
        .astype(jnp.bfloat16)
    )
    mixed = hidden_in + jnp.dot(
        lax.all_gather(attn, "et", axis=1, tiled=True), out_proj, preferred_element_type=jnp.float32
    )
    squares = lax.psum(jnp.sum(mixed * mixed, axis=1), "et")
    normed = (mixed * lax.rsqrt(squares / D + epsilon)[:, None] * norm_gain[None, :]).astype(
        jnp.bfloat16
    )
    capacity = CAP
    flat_ids = expert_ids.reshape(-1)
    flat_weights = route_weights.reshape(-1)
    in_window = flat_ids < experts_here
    onehot = (flat_ids[:, None] == jnp.arange(experts_here, dtype=jnp.int32)[None, :]).astype(
        jnp.int32
    )
    before = jnp.cumsum(onehot, axis=0) - onehot
    slot_index = jnp.sum(before * onehot, axis=1)
    target = jnp.where(in_window, flat_ids * capacity + slot_index, experts_here * capacity)
    token_of = jnp.arange(flat_ids.shape[0], dtype=jnp.int32) // expert_ids.shape[1]
    source_table = (
        jnp.full((experts_here * capacity,), tok_rows, jnp.int32)
        .at[target]
        .set(token_of, mode="drop")
    )
    slot_total = experts_here * capacity
    full_rows = lax.all_gather(normed, "et", axis=1, tiled=True)
    padded = jnp.concatenate([full_rows, jnp.zeros((1, full_rows.shape[1]), jnp.bfloat16)], axis=0)
    outgoing = padded[source_table].reshape(experts_here, capacity, full_rows.shape[1])
    arrived = lax.all_to_all(outgoing, "ctx", split_axis=0, concat_axis=0, tiled=True).reshape(
        slot_total, full_rows.shape[1]
    )
    gate_pre = jnp.dot(arrived, w_gate[0], preferred_element_type=jnp.float32)
    up_pre = jnp.dot(arrived, w_up[0], preferred_element_type=jnp.float32)
    activated = (jax.nn.silu(gate_pre) * up_pre).astype(jnp.bfloat16)
    partial_out = jnp.dot(activated, w_down[0], preferred_element_type=jnp.float32)
    expert_out = lax.psum_scatter(
        partial_out.astype(jnp.bfloat16), "et", scatter_dimension=1, tiled=True
    ).astype(jnp.float32)
    out_cols = expert_out.shape[1]
    returned = lax.all_to_all(
        expert_out.reshape(experts_here, capacity, out_cols).astype(jnp.bfloat16),
        "ctx",
        split_axis=0,
        concat_axis=0,
        tiled=True,
    ).astype(jnp.float32)
    flat_back = jnp.concatenate(
        [returned.reshape(slot_total, out_cols), jnp.zeros((1, out_cols), jnp.float32)], axis=0
    )
    picked = flat_back[target] * flat_weights[:, None]
    combined = jnp.sum(picked.reshape(tok_rows, expert_ids.shape[1], out_cols), axis=1)
    return mixed + combined


def solution(mesh):
    return jax.shard_map(
        body,
        mesh=mesh,
        in_specs=(
            P("ctx", "et"),
            P("ctx", "et"),
            P("ctx", None),
            P("ctx", None),
            P(None, "et"),
            P("et"),
            P("ctx", None),
            P("ctx", None),
            P("ctx", None, "et"),
            P("ctx", None, "et"),
            P("ctx", "et", None),
        ),
        out_specs=P("ctx", "et"),
        check_vma=False,
    )
```

profile of v0, /device:TPU:28, one launch (start us, length us, event | category | flops | bytes accessed | tf_op | source)
XLA Modules:
  0.0 224.6 jit_solution(3778753503196402284)
XLA Ops:
  6.5 0.0 copy-start
  6.5 0.0 all-gather.3.cloned.1.call-start
  6.5 0.9 constant_dynamic-slice_fusion.1
  7.5 0.8 constant_dynamic-slice_fusion
  8.3 0.1 copy.25
  8.4 0.1 iota_compare_fusion
  8.5 25.0 %all_gather.13 = bf16[1024,128]{0,1:T(8,128)(2,1)S(1)} all-gather(bf16[128,128]{0,1:T(8,128)(2,1)S(1)} %copy.25), channel_id=1, replica_groups=mesh['ctx'=8,'et'=4] {'ctx'}, dimensions={0}, use_global_device_ids=true | all-gather | bytes 294912 | tf_op jit(solution)/shard_map/all_gather | solution.py:44
  33.5 30.8 %all_gather.12 = bf16[1024,128]{1,0:T(8,128)(2,1)S(1)} all-gather(bf16[128,128]{1,0:T(8,128)(2,1)S(1)} %constant_dynamic-slice_fusion.1), channel_id=1, replica_groups=mesh['ctx'=8,'et'=4] {'ctx'}, dimensions={0}, use_global_device_ids=true | all-gather | bytes 294912 | tf_op jit(solution)/shard_map/all_gather | solution.py:43
  64.3 1.7 fusion.1
  66.1 1.0 fusion.7
  67.1 0.0 copy-start.2
  67.1 1.9 fusion.26
  69.0 0.0 all-gather.3.cloned.1.call-update
  69.0 0.0 all-gather.5.cloned.1.call-start
  69.0 0.0 copy-done.2
  69.0 0.1 copy.21
  69.1 0.1 eq.29
  69.2 0.1 eq.25
  69.3 0.1 copy.19
  69.5 0.1 lt.48
  69.6 0.0 copy-start.3
  69.6 17.2 %all-gather.3.cloned.1.call-done = bf16[128,4096]{0,1:T(8,128)(2,1)} async-done(((bf16[128,1024]{0,1:T(8,128)(2,1)}), bf16[128,4096]{0,1:T(8,128)(2,1)}) %all-gather.3.cloned.1.call-update) | async-done | bytes 1048592 | tf_op jit(solution)/shard_map/all_gather | solution.py:65
  86.8 5.8 %multiply_reduce_fusion = (f32[128]{0:T(128)S(1)}, f32[128,1024]{1,0:T(8,128)}) fusion(f32[128,1024]{1,0:T(8,128)} %param.11, bf16[128,4096]{0,1:T(8,128)(2,1)} %all-gather.3.cloned.1.call-done, bf16[4096,1024]{1,0:T(8,128)(2,1)} %param.15), kind=kOutput, calls=%fused_computation.25 | convolution fusion | flops 1074134912 | bytes 10486272 | tf_op jit(solution)/shard_map/dot_general | solution.py:64
  92.6 6.0 %psum.7 = f32[128]{0:T(128)S(1)} all-reduce(f32[128]{0:T(128)S(1)} %get-tuple-element.9), channel_id=1, replica_groups=mesh['ctx'=8,'et'=4] {'et'}, use_global_device_ids=true, to_apply=%region_3.4 | all-reduce | flops 128 | bytes 1024 | tf_op jit(solution)/shard_map/psum | solution.py:67
  98.6 0.0 copy-done.3
  98.6 1.9 multiply_convert_fusion
  100.5 0.0 all-gather.5.cloned.1.call-update
  100.5 0.0 reduce-scatter.2.cloned.1.call-start
  100.6 0.1 copy.20
  100.7 0.1 mul.90
  100.8 2.3 %reduce-window.6 = s32[8,8,128]{2,1,0:T(8,128)S(1)} reduce-window(s32[8,8,128]{2,1,0:T(8,128)S(1)} %fusion.43, s32[]{:T(128)} %constant.33.clone.1), window={size=1x1x128 pad=0_0x0_0x127_0}, to_apply=%region_4.5 | reduce-window | flops 1040384 | bytes 65540 | tf_op jit(solution)/shard_map/reduce-window
  103.0 0.3 slice_reduce_fusion
  103.3 0.2 reduce-window.9
  103.5 0.1 add_bitcast_fusion
  103.6 4.3 %scatter_custom_fusion = s32[96]{0:T(128)S(1)} fusion(s32[1024]{0:T(1024)S(1)} %bitcast.92, s32[1024]{0:T(1024)S(1)} %add_select_fusion, s32[]{:T(128)} %constant.32.clone.1), kind=kCustom, calls=%fused_computation.68 | custom fusion | bytes 388 | tf_op jit(solution)/shard_map/scatter | solution.py:85
  108.0 10.3 %all-gather.5.cloned.1.call-done = bf16[128,4096]{1,0:T(8,128)(2,1)} async-done(((bf16[128,1024]{1,0:T(8,128)(2,1)}), bf16[128,4096]{1,0:T(8,128)(2,1)}) %all-gather.5.cloned.1.call-update) | async-done | bytes 1048592 | tf_op jit(solution)/shard_map/all_gather | solution.py:88
  118.3 2.3 %concatenate.8 = bf16[129,4096]{1,0:T(8,128)(2,1)} pad(bf16[128,4096]{1,0:T(8,128)(2,1)} %all-gather.5.cloned.1.call-done, bf16[]{:T(256)} %constant.76.clone.1), padding=0_1x0_0 | pad | bytes 2105346 | tf_op jit(solution)/shard_map/concatenate | solution.py:89
  120.6 4.1 %gather_fusion = bf16[96,4096]{1,0:T(8,128)(2,1)} fusion(bf16[129,4096]{1,0:T(8,128)(2,1)} %concatenate.8, s32[1024]{0:T(1024)S(1)} %pad_clamp_fusion), kind=kCustom, calls=%fused_computation | custom fusion | bytes 1573248 | tf_op jit(solution)/shard_map/gather | solution.py:90
  124.7 2.2 reshape.137
  126.9 29.9 %all_to_all.10 = bf16[8,12,4096]{2,1,0:T(8,128)(2,1)} all-to-all(bf16[8,12,4096]{2,1,0:T(8,128)(2,1)} %reshape.137), channel_id=1, replica_groups=mesh['ctx'=8,'et'=4] {'ctx'}, dimensions={0} | all-to-all | bytes 1572864 | tf_op jit(solution)/shard_map/all_to_all | solution.py:91
  156.8 2.2 reshape.138
  158.9 2.8 %fusion.5 = f32[96,384]{1,0:T(8,128)S(1)} fusion(bf16[96,4096]{1,0:T(8,128)(2,1)} %reshape.138, bf16[1,4096,384]{2,1,0:T(8,128)(2,1)} %param.19), kind=kOutput, calls=%fused_computation.12 | convolution fusion | flops 301989888 | bytes 4079616 | tf_op jit(solution)/shard_map/dot_general | solution.py:94
  161.7 0.0 copy-done
  161.7 0.0 copy-start.4
  161.7 4.5 %convolution_convert_fusion = bf16[96,4096]{1,0:T(8,128)(2,1)} fusion(bf16[1,384,4096]{2,1,0:T(8,128)(2,1)S(1)} %copy-done, bf16[96,4096]{1,0:T(8,128)(2,1)} %reshape.138, bf16[1,4096,384]{2,1,0:T(8,128)(2,1)} %param.20, f32[96,384]{1,0:T(8,128)S(1)} %fusion.5), kind=kOutput, calls=%fused_computation.3 | convolution fusion | flops 604594176 | bytes 8011776 | tf_op jit(solution)/shard_map/dot_general | solution.py:97
  166.2 0.0 reduce-scatter.2.cloned.1.call-update
  166.3 23.4 %reduce-scatter.2.cloned.1.call-done = bf16[96,1024]{1,0:T(8,128)(2,1)} async-done(((bf16[96,4096]{1,0:T(8,128)(2,1)}), bf16[96,1024]{1,0:T(8,128)(2,1)}) %reduce-scatter.2.cloned.1.call-update) | async-done | bytes 196624 | tf_op jit(solution)/shard_map/reduce_scatter | solution.py:98
  189.7 1.7 convert_element_type.39
  191.3 6.0 %all-to-all-start.1 = ((bf16[8,12,1024]{2,1,0:T(8,128)(2,1)}), bf16[8,12,1024]{2,1,0:T(8,128)(2,1)S(1)}, u32[]{:S(2)}, u32[]{:S(2)}) async-start(bf16[8,12,1024]{2,1,0:T(8,128)(2,1)} %convert_element_type.39), calls=%async_computation.2 | async-start | bytes 524288 | tf_op jit(solution)/shard_map/all_to_all | solution.py:102
  197.3 0.0 copy-done.4
  197.3 0.1 copy.23
  197.5 6.4 %all-to-all-done.1 = bf16[8,12,1024]{2,1,0:T(8,128)(2,1)S(1)} async-done(((bf16[8,12,1024]{2,1,0:T(8,128)(2,1)}), bf16[8,12,1024]{2,1,0:T(8,128)(2,1)S(1)}, u32[]{:S(2)}, u32[]{:S(2)}) %all-to-all-start.1) | async-done | bytes 196640 | tf_op jit(solution)/shard_map/all_to_all | solution.py:102
  203.9 0.7 reshape.139
  204.6 1.7 pad_convert_fusion
  206.3 7.4 %gather_fusion.1 = f32[1024,1024]{1,0:T(8,128)} fusion(f32[97,1024]{1,0:T(8,128)} %pad_convert_fusion, s32[1024]{0:T(1024)S(1)} %broadcast_clamp_fusion), kind=kCustom, calls=%fused_computation.1 | custom fusion | bytes 8392704 | tf_op jit(solution)/shard_map/gather | solution.py:112
  213.7 0.0 copy-start.1
  213.7 3.5 %fusion = f32[128,1024]{1,0:T(8,128)S(1)} fusion(f32[1024,1024]{1,0:T(8,128)} %gather_fusion.1, f32[128,8]{1,0:T(8,128)S(1)} %copy.23), kind=kLoop, calls=%fused_computation.5 | loop fusion | flops 1966080 | bytes 4722688 | tf_op jit(solution)/shard_map/reduce_sum | solution.py:113
  217.2 0.0 copy-done.1
  217.2 0.9 add.97
  (12 shorter events, 0.1 us)
Async XLA Ops:
  6.5 155.2 %copy-start = (bf16[1,384,4096]{2,1,0:T(8,128)(2,1)S(1)}, bf16[1,384,4096]{2,1,0:T(8,128)(2,1)}, u32[]{:S(2)}) copy-start(bf16[1,384,4096]{2,1,0:T(8,128)(2,1)} %param.21) | copy-start | bytes 9437188
  6.5 80.3 %all-gather.3.cloned.1.call-start = ((), (), s32[]{:S(2)}) async-start(), calls=%async_computation.3 | async-start | bytes 1310720 | tf_op jit(solution)/shard_map/all_gather | solution.py:65
  67.1 2.0 copy-start.2
  69.0 49.3 %all-gather.5.cloned.1.call-start = ((), (), s32[]{:S(2)}) async-start(), calls=%async_computation.4 | async-start | bytes 1310720 | tf_op jit(solution)/shard_map/all_gather | solution.py:88
  69.6 29.0 %copy-start.3 = (f32[1024]{0:T(1024)S(1)}, f32[1024]{0:T(1024)}, u32[]{:S(2)}) copy-start(f32[1024]{0:T(1024)} %param.16) | copy-start | bytes 12292
  100.5 89.2 %reduce-scatter.2.cloned.1.call-start = ((), (), s32[]{:S(2)}) async-start(), calls=%async_computation.5 | async-start | bytes 983040 | tf_op jit(solution)/shard_map/reduce_scatter | solution.py:98
  161.7 35.6 %copy-start.4 = (f32[128,8]{0,1:T(8,128)S(1)}, f32[128,8]{0,1:T(8,128)}, u32[]{:S(2)}) copy-start(f32[128,8]{0,1:T(8,128)} %param.18) | copy-start | bytes 12292
  191.3 12.5 %all-to-all-start.1 = ((bf16[8,12,1024]{2,1,0:T(8,128)(2,1)}), bf16[8,12,1024]{2,1,0:T(8,128)(2,1)S(1)}, u32[]{:S(2)}, u32[]{:S(2)}) async-start(bf16[8,12,1024]{2,1,0:T(8,128)(2,1)} %convert_element_type.39), calls=%async_computation.2 | async-start | bytes 524288 | tf_op jit(solution)/shard_map/all_to_all | solution.py:102
  213.7 3.5 %copy-start.1 = (f32[128,1024]{1,0:T(8,128)S(1)}, f32[128,1024]{1,0:T(8,128)}, u32[]{:S(2)}) copy-start(f32[128,1024]{1,0:T(8,128)} %get-tuple-element.10) | copy-start | bytes 1572868
Sparse Core Ops, SparseCore 0:
  69.1 17.6 all-gather.2
  100.6 17.6 all-gather.4
  166.4 23.2 reduce-scatter.1
where the time goes:
time: 229 us; the launch traced here: 225 us
  blocking collectives  91.7 us (40%)
  waiting for transfers between devices  57.4 us (25%)
  local copies, waits for them, and re-layouts  27.8 us (12%)
  matrix products  16.7 us (7%)
  between operations  13.3 us (6%)
  other arithmetic  11.6 us (5%)
  starting transfers between devices  6.08 us (3%)
    all_gather x1, blocking collectives, body(): key_piece = lax.all_gather(key_local, 'ctx', axis=0, tiled=True)  30.8 us
    all_to_all x1, blocking collectives, body(): lax.all_to_all(outgoing, 'ctx', split_axis=0, concat_axis=0, tiled=True)  29.9 us
    all_gather x1, blocking collectives, body(): value_piece = lax.all_gather(value_local, 'ctx', axis=0, tiled=True)  25 us
    reduce_scatter x1, waiting for transfers between devices, body(): lax.psum_scatter(partial_out.astype(jnp.bfloat16), 'et', scatter_dimensio...  23.4 us
    all_gather x1, waiting for transfers between devices, body(): lax.all_gather(attn, 'et', axis=1, tiled=True)  17.2 us
    all_gather x1, waiting for transfers between devices, body(): full_rows = lax.all_gather(normed, 'et', axis=1, tiled=True)  10.3 us
    gather x1, local copies, waits for them, and re-layouts, body(): picked = flat_back[target] * flat_weights[:, None]  7.41 us
    all_to_all x1, waiting for transfers between devices, body(): lax.all_to_all(expert_out.reshape(experts_here, capacity, out_cols).astyp...  6.4 us
  transfers between devices with their start and end apart: 4, of which 4 were waited for; matrix products, arithmetic and copies ran while one was open for 4% of the time, Pallas kernels for 0%

commit v1 on v0

v1 whole, which is shorter than its diff:
```python
import functools
import math

import jax
import jax.numpy as jnp
from jax import lax
from jax.experimental import pallas as pl
from jax.experimental.pallas import tpu as pltpu
from jax.sharding import PartitionSpec as P

D = 4096
HEADS = 32
KV_HEADS = 2
HD = 128
SLOT = 16
EXTRA = 128

epsilon = 1e-06
masked_score = -1e30
BF = jnp.bfloat16
F32 = jnp.float32


def dot(a, b):
    return jnp.dot(a, b, preferred_element_type=F32)


def kernel(
    n, m, AC, NR,
    hidden, queries, keys, values, out_proj, gain, ids, weights, w_gate, w_up, w_down,
    out,
    q_v, kv, wo, wg, wu, wd, hid,
    m_s, acc_s, att, xe, outb, arr, selw, pdown, pin, mine, xs, xin, eo, ret,
    lsem, kv_s, kv_r, kvf_s, kvf_r, att_s, att_r, attf_s,
    d_s, d_r, g_s, g_r, gf_s, p_s, p_r, x_s, x_r, r_s, r_r,
):
    T, F = hidden.shape
    LH = F // HD
    group = HEADS // KV_HEADS
    C = n * SLOT
    U = w_gate.shape[2]
    chips = m // 2
    c = lax.axis_index("ctx")
    j = lax.axis_index("et")
    p = lax.rem(j, 2)
    chip = lax.div(j, 2)
    sib = j + 1 - 2 * p
    kvh = lax.div(j * LH, group)
    head_lanes = pl.ds(pl.multiple_of(kvh * HD, HD), HD)

    def other(o):
        return lax.rem(chip + o, chips)

    def remote(src, dst, ssem, rsem, dc, dj):
        return pltpu.make_async_remote_copy(
            src_ref=src, dst_ref=dst, send_sem=ssem, recv_sem=rsem,
            device_id=(dc, dj), device_id_type=pl.DeviceIdType.MESH,
        )

    def loop(lo, hi, f):
        def step(i, carry):
            f(i)
            return carry
        lax.fori_loop(lo, hi, step, 0)

    local = [
        pltpu.make_async_copy(keys.at[:, head_lanes], kv.at[c, :, pl.ds(0, HD)], lsem.at[0]),
        pltpu.make_async_copy(values.at[:, head_lanes], kv.at[c, :, pl.ds(HD, HD)], lsem.at[1]),
        pltpu.make_async_copy(queries, q_v, lsem.at[2]),
        pltpu.make_async_copy(hidden, hid, lsem.at[3]),
        pltpu.make_async_copy(out_proj, wo, lsem.at[4]),
        pltpu.make_async_copy(w_gate.at[0], wg, lsem.at[5]),
        pltpu.make_async_copy(w_up.at[0], wu, lsem.at[6]),
        pltpu.make_async_copy(w_down.at[0], wd, lsem.at[7]),
    ]
    for copy in local[:3]:
        copy.start()

    barrier = pltpu.get_barrier_semaphore()
    for o in range(1, n):
        pl.semaphore_signal(barrier, inc=1, device_id=(lax.rem(c + o, n), j), device_id_type=pl.DeviceIdType.MESH)
    for o in range(1, m):
        pl.semaphore_signal(barrier, inc=1, device_id=(c, lax.rem(j + o, m)), device_id_type=pl.DeviceIdType.MESH)
    for copy in local[3:]:
        copy.start()
    ones = jnp.ones((T, HD), BF)
    for s in range(n):
        kv[s, :, 2 * HD:] = ones
    local[0].wait()
    local[1].wait()
    pl.semaphore_wait(barrier, n - 1 + m - 1)

    def half(s, which):
        return kv.at[s, :, pl.ds(pl.multiple_of(which * HD, HD), HD)]

    def kv_send(o):
        d = c + o
        @pl.when(d < n)
        def _():
            remote(half(c, p), half(c, p), kv_s.at[o], kv_r.at[c], d, j).start()
    loop(1, n, kv_send)

    col = lax.broadcasted_iota(jnp.int32, (T, C), 1)
    expert_col = lax.div(col, SLOT)
    slot_col = lax.rem(col, SLOT)
    hit = jnp.zeros((T, C), F32)
    weight = jnp.zeros((T, C), F32)
    for k in range(ids.shape[1]):
        same = ids[:, k : k + 1] == expert_col
        hit = hit + jnp.where(same, 1.0, 0.0)
        weight = weight + jnp.where(same, weights[:, k : k + 1], 0.0)
    row_t = lax.broadcasted_iota(jnp.int32, (T, T), 0)
    col_t = lax.broadcasted_iota(jnp.int32, (T, T), 1)
    earlier = jnp.where(col_t < row_t, 1.0, 0.0).astype(BF)
    before = dot(earlier, hit.astype(BF))
    chosen = jnp.where((before == slot_col.astype(F32)) & (hit > 0.5), 1.0, 0.0)
    weight = weight * chosen
    w_hi = weight.astype(BF)
    selw[0] = w_hi
    selw[1] = (weight - w_hi.astype(F32)).astype(BF)
    sel = chosen.T.astype(BF)

    factor = math.log2(math.e) / math.sqrt(HD)
    causal = col_t <= row_t
    local[2].wait()

    def block(s, first):
        k_blk = kv[s, :, :HD]
        v_blk = kv[s, :, HD:]
        for h in range(LH):
            q_h = q_v[:, h * HD : (h + 1) * HD]
            sc = lax.dot_general(q_h, k_blk, (((1,), (1,)), ((), ())), preferred_element_type=F32)
            if first:
                sc = jnp.where(causal, sc, masked_score)
                top = jnp.broadcast_to(jnp.max(sc, axis=1, keepdims=True), (T, HD))
                pr = jnp.where(causal, jnp.exp2((sc - top) * factor), 0.0)
                acc_s[h] = dot(pr.astype(BF), v_blk)
            else:
                old = m_s[h]
                top = jnp.maximum(old, jnp.max(sc, axis=1, keepdims=True))
                pr = jnp.exp2((sc - top) * factor)
                keep = jnp.exp2((old - top) * factor)
                acc_s[h] = acc_s[h] * jnp.concatenate([keep, keep], axis=1) + dot(pr.astype(BF), v_blk)
            m_s[h] = top

    block(c, True)

    def kv_step(o):
        s = c - o
        @pl.when(s >= 0)
        def _():
            remote(half(s, p), half(s, p), kv_s.at[o], kv_r.at[s], c, sib).wait_recv()
            remote(half(s, p), half(s, p), kvf_s.at[s], kvf_r.at[s], c, sib).start()
        prev = s + 1
        @pl.when((prev >= 0) & (o > 1))
        def _():
            remote(half(prev, 1 - p), half(prev, 1 - p), kvf_s.at[prev], kvf_r.at[prev], c, sib).wait_recv()
            block(prev, False)
    loop(1, n + 1, kv_step)

    for h in range(LH):
        att[j, :, h * HD : (h + 1) * HD] = (acc_s[h, :, :HD] / acc_s[h, :, HD:]).astype(BF)
    FC = F // AC

    def piece(jj, k):
        return att.at[jj, :, pl.ds(k * FC, FC)]

    for k in range(AC):
        for o in range(1, chips):
            t = other(o) * 2 + p
            remote(piece(j, k), piece(j, k), att_s.at[t, k], att_r.at[j, k], c, t).start()
        remote(piece(j, k), piece(j, k), att_s.at[sib, k], att_r.at[j, k], c, sib).start()

    local[3].wait()
    local[4].wait()

    def project(jj, k):
        return dot(att[jj, :, k * FC : (k + 1) * FC], wo[pl.ds(pl.multiple_of(jj * F + k * FC, FC), FC), :])

    out[...] = hid[...] + dot(att[j], wo[pl.ds(pl.multiple_of(j * F, F), F), :])
    for k in range(AC):
        remote(piece(sib, k), piece(sib, k), att_s.at[sib, k], att_r.at[sib, k], c, sib).wait_recv()
    if chips == 1:
        out[...] += dot(att[sib], wo[pl.ds(pl.multiple_of(sib * F, F), F), :])
    for o in range(1, chips):
        t = other(o) * 2 + p
        for k in range(AC):
            remote(piece(t, k), piece(t, k), att_s.at[t, k], att_r.at[t, k], c, sib).wait_recv()
            remote(piece(t, k), piece(t, k), attf_s.at[t, k], att_r.at[t, k], c, sib).start()
            if o == 1:
                out[...] += project(sib, k)
        out[...] += dot(att[t], wo[pl.ds(pl.multiple_of(t * F, F), F), :])
    for o in range(1, chips):
        t = other(o) * 2 + 1 - p
        for k in range(AC):
            remote(piece(t, k), piece(t, k), att_s.at[t, k], att_r.at[t, k], c, sib).wait_recv()
        out[...] += dot(att[t], wo[pl.ds(pl.multiple_of(t * F, F), F), :])

    mixed = out[...]
    xe[:, :F] = (mixed * gain[...]).astype(BF)
    squares = jnp.sum(mixed * mixed, axis=1, keepdims=True)
    part0 = squares.astype(BF).astype(F32)
    part1 = (squares - part0).astype(BF).astype(F32)
    part2 = squares - part0 - part1
    lane = lax.broadcasted_iota(jnp.int32, (T, EXTRA), 1)
    xe[:, F:] = jnp.where(
        lane == 0, part0, jnp.where(lane == 1, part1, jnp.where(lane == 2, part2, 0.0))
    ).astype(BF)
    outb[...] = dot(sel, xe[...]).astype(BF).reshape(n, SLOT, F + EXTRA)

    def d_send(o):
        d = lax.rem(c + o, n)
        remote(outb.at[d], arr.at[j, c], d_s.at[o], d_r.at[c], d, j).start()
    loop(1, n, d_send)
    arr[j, c] = outb[c]

    def spread(s):
        for o in range(1, chips):
            t = other(o) * 2 + p
            remote(arr.at[j, s], arr.at[j, s], g_s.at[t, s], g_r.at[j, s], c, t).start()
        remote(arr.at[j, s], arr.at[j, s], g_s.at[sib, s], g_r.at[j, s], c, sib).start()

    def d_step(o):
        s = lax.rem(c + n - o, n)
        @pl.when(o > 0)
        def _():
            remote(outb.at[s], arr.at[j, s], d_s.at[o], d_r.at[s], c, sib).wait_recv()
        spread(s)
    loop(0, n, d_step)

    for i in range(5, 8):
        local[i].wait()

    def rows_of(t):
        return arr[t].reshape(C, F + EXTRA)

    def pre(t):
        x = rows_of(t)
        at = pl.ds(pl.multiple_of(t * F, F), F)
        sq = jnp.sum(x[:, F:].astype(F32), axis=1, keepdims=True)
        return dot(x[:, :F], wg[at, :]), dot(x[:, :F], wu[at, :]), sq

    gate, up, sq = pre(j)

    def add(t, gate, up, sq):
        g1, u1, s1 = pre(t)
        return gate + g1, up + u1, sq + s1

    for o in range(1, chips):
        t = other(o) * 2 + p
        def g_step(i):
            s = lax.rem(c + n - i, n)
            remote(arr.at[t, s], arr.at[t, s], g_s.at[t, s], g_r.at[t, s], c, sib).wait_recv()
            remote(arr.at[t, s], arr.at[t, s], gf_s.at[t, s], g_r.at[t, s], c, sib).start()
        loop(0, n, g_step)

    def g_wait(t):
        def step(s):
            remote(arr.at[t, s], arr.at[t, s], g_s.at[t, s], g_r.at[t, s], c, sib).wait_recv()
        loop(0, n, step)

    g_wait(sib)
    gate, up, sq = add(sib, gate, up, sq)
    for o in range(1, chips):
        gate, up, sq = add(other(o) * 2 + p, gate, up, sq)
    for o in range(1, chips):
        t = other(o) * 2 + 1 - p
        g_wait(t)
        gate, up, sq = add(t, gate, up, sq)
    scale = lax.rsqrt(sq / D + epsilon)
    gate = gate * scale
    up = up * scale
    act = (gate / (1.0 + jnp.exp(-gate)) * up).astype(BF)

    CR = C // NR
    NC = n // NR

    def down(t, r):
        return dot(act[r * CR : (r + 1) * CR], wd[:, pl.ds(pl.multiple_of(t * F, F), F)])

    def at_rows(r):
        return pl.ds(r * CR, CR)

    def pair(r, q):
        return remote(pdown.at[q, at_rows(r)], pin.at[q, at_rows(r)], p_s.at[q, r], p_r.at[q, r], c, sib)

    def cross(r, o):
        q = other(o)
        return remote(xs.at[q, at_rows(r)], xin.at[chip, at_rows(r)], x_s.at[q, r], x_r.at[chip, r], c, q * 2 + p)

    for r in range(NR):
        for o in list(range(1, chips)) + [0]:
            q = other(o)
            pdown[q, r * CR : (r + 1) * CR] = down(q * 2 + 1 - p, r).astype(BF)
            pair(r, q).start()
    for r in range(NR):
        rr = slice(r * CR, (r + 1) * CR)
        for o in range(1, chips):
            q = other(o)
            part = down(q * 2 + p, r).astype(BF).astype(F32)
            pair(r, q).wait_recv()
            xs[q, rr] = (part + pin[q, rr].astype(F32)).astype(BF)
            cross(r, o).start()
    for r in range(NR):
        rr = slice(r * CR, (r + 1) * CR)
        mine[rr] = down(chip * 2 + p, r).astype(BF).astype(F32)
        pair(r, chip).wait_recv()
        mine[rr] += pin[chip, rr].astype(F32)
    for r in range(NR):
        rr = slice(r * CR, (r + 1) * CR)
        total = mine[rr]
        for o in range(1, chips):
            q = other(o)
            remote(xin.at[q, at_rows(r)], xin.at[q, at_rows(r)], x_s.at[q, r], x_r.at[q, r], c, sib).wait_recv()
            total = total + xin[q, rr].astype(F32)
        eo[r * NC : (r + 1) * NC] = total.astype(BF).reshape(NC, SLOT, F)

        def r_send(s):
            @pl.when(s != c)
            def _():
                remote(eo.at[s], ret.at[c], r_s.at[s], r_r.at[c], s, j).start()
            @pl.when(s == c)
            def _():
                ret[c] = eo[c]
        loop(r * NC, (r + 1) * NC, r_send)

    def r_wait(s):
        @pl.when(s != c)
        def _():
            remote(eo.at[s], ret.at[s], r_s.at[s], r_r.at[s], s, j).wait_recv()
    loop(0, n, r_wait)
    back = ret[...].reshape(C, F)
    out[...] += dot(selw[0], back) + dot(selw[1], back)

    def kv_done(o):
        @pl.when(c + o < n)
        def _():
            remote(half(c, p), half(c, p), kv_s.at[o], kv_r.at[c], c, sib).wait_send()
        @pl.when(c - o >= 0)
        def _():
            s = c - o
            remote(half(s, p), half(s, p), kvf_s.at[s], kvf_r.at[s], c, sib).wait_send()
        remote(outb.at[o], arr.at[j, c], d_s.at[o], d_r.at[c], c, sib).wait_send()
    loop(1, n, kv_done)

    def rest_done(s):
        for o in range(1, chips):
            t = other(o) * 2 + p
            remote(arr.at[j, s], arr.at[j, s], g_s.at[t, s], g_r.at[j, s], c, t).wait_send()
            remote(arr.at[t, s], arr.at[t, s], gf_s.at[t, s], g_r.at[t, s], c, sib).wait_send()
        remote(arr.at[j, s], arr.at[j, s], g_s.at[sib, s], g_r.at[j, s], c, sib).wait_send()
        @pl.when(s != c)
        def _():
            remote(eo.at[s], ret.at[c], r_s.at[s], r_r.at[c], s, j).wait_send()
    loop(0, n, rest_done)
    for k in range(AC):
        for o in range(1, chips):
            t = other(o) * 2 + p
            remote(piece(j, k), piece(j, k), att_s.at[t, k], att_r.at[j, k], c, t).wait_send()
            remote(piece(t, k), piece(t, k), attf_s.at[t, k], att_r.at[t, k], c, sib).wait_send()
        remote(piece(j, k), piece(j, k), att_s.at[sib, k], att_r.at[j, k], c, sib).wait_send()
    for r in range(NR):
        for o in range(chips):
            pair(r, other(o)).wait_send()
        for o in range(1, chips):
            cross(r, o).wait_send()


def body(hidden, queries, keys, values, out_proj, gain, ids, weights, w_gate, w_up, w_down):
    n = lax.axis_size("ctx")
    m = lax.axis_size("et")
    T, F = hidden.shape
    U = w_gate.shape[2]
    LH = F // HD
    C = n * SLOT
    chips = m // 2
    AC = 4 if F % 512 == 0 else 2
    NR = 2
    DMA = pltpu.SemaphoreType.DMA
    V = pltpu.VMEM
    any_ = pl.BlockSpec(memory_space=pl.ANY)
    vm = pl.BlockSpec(memory_space=pltpu.VMEM)
    return pl.pallas_call(
        functools.partial(kernel, n, m, AC, NR),
        out_shape=jax.ShapeDtypeStruct((T, F), F32),
        in_specs=[any_, any_, any_, any_, any_, vm, vm, vm, any_, any_, any_],
        out_specs=vm,
        scratch_shapes=[
            V((T, F), BF),
            V((n, T, 3 * HD), BF),
            V(out_proj.shape, BF),
            V(w_gate.shape[1:], BF),
            V(w_up.shape[1:], BF),
            V(w_down.shape[1:], BF),
            V((T, F), F32),
            V((LH, T, HD), F32),
            V((LH, T, 2 * HD), F32),
            V((m, T, F), BF),
            V((T, F + EXTRA), BF),
            V((n, SLOT, F + EXTRA), BF),
            V((m, n, SLOT, F + EXTRA), BF),
            V((2, T, C), BF),
            V((chips, C, F), BF),
            V((chips, C, F), BF),
            V((C, F), F32),
            V((chips, C, F), BF),
            V((chips, C, F), BF),
            V((n, SLOT, F), BF),
            V((n, SLOT, F), BF),
            DMA((8,)),
            DMA((n,)), DMA((n,)), DMA((n,)), DMA((n,)),
            DMA((m, AC)), DMA((m, AC)), DMA((m, AC)),
            DMA((n,)), DMA((n,)),
            DMA((m, n)), DMA((m, n)), DMA((m, n)),
            DMA((chips, NR)), DMA((chips, NR)),
            DMA((chips, NR)), DMA((chips, NR)),
            DMA((n,)), DMA((n,)),
        ],
        compiler_params=pltpu.CompilerParams(
            collective_id=0, has_side_effects=True, vmem_limit_bytes=58 * 1024 * 1024
        ),
        cost_estimate=pl.CostEstimate(flops=4 * 10**9, bytes_accessed=2 * 10**7, transcendentals=10**6),
    )(
        hidden, queries, keys, values, out_proj, gain.reshape(1, F), ids, weights,
        w_gate, w_up, w_down,
    )


def solution(mesh):
    return jax.shard_map(
        body,
        mesh=mesh,
        in_specs=(
            P("ctx", "et"),
            P("ctx", "et"),
            P("ctx", None),
            P("ctx", None),
            P(None, "et"),
            P("et"),
            P("ctx", None),
            P("ctx", None),
            P("ctx", None, "et"),
            P("ctx", None, "et"),
            P("ctx", "et", None),
        ),
        out_specs=P("ctx", "et"),
        check_vma=False,
    )
```

time: 229 us -> 68.7 us (0.30); the launches traced: 225 us -> 68.4 us
  blocking collectives: 91.7 us -> 0 us
  Pallas kernels: 0 us -> 63.7 us
  waiting for transfers between devices: 57.4 us -> 0 us
  local copies, waits for them, and re-layouts: 27.8 us -> 4.71 us
  matrix products: 16.7 us -> 0 us
  between operations: 13.3 us -> 0.01 us
  other arithmetic: 11.6 us -> 0 us
  starting transfers between devices: 6.08 us -> 0 us
    pallas_call x0 -> x1, Pallas kernels: none -> 63.7 us  [body(): pl.pallas_call(functools.partial(kernel, n, m, AC, NR), out_shape=jax.Sha...]
    all_gather x2 -> x0, blocking collectives: 55.9 us -> none  [the longest x1 30.8 us: body(): key_piece = lax.all_gather(key_local, 'ctx', axis=0, tiled=True)]
    all_to_all x1 -> x0, blocking collectives: 29.9 us -> none  [body(): lax.all_to_all(outgoing, 'ctx', split_axis=0, concat_axis=0, tiled=True)]
    all_gather x2 -> x0, waiting for transfers between devices: 27.6 us -> none  [the longest x1 17.2 us: body(): lax.all_gather(attn, 'et', axis=1, tiled=True)]
    reduce_scatter x1 -> x0, waiting for transfers between devices: 23.4 us -> none  [body(): lax.psum_scatter(partial_out.astype(jnp.bfloat16), 'et', scatter_dimensio...]
    dot_general x5 -> x0, matrix products: 16.7 us -> none  [the longest x1 5.8 us: body(): jnp.dot(lax.all_gather(attn, 'et', axis=1, tiled=True), out_proj, preferr...]
    gather x2 -> x0, local copies, waits for them, and re-layouts: 11.5 us -> none  [the longest x1 7.41 us: body(): picked = flat_back[target] * flat_weights[:, None]]
    all_to_all x1 -> x0, waiting for transfers between devices: 6.4 us -> none  [body(): lax.all_to_all(expert_out.reshape(experts_here, capacity, out_cols).astyp...]
  transfers between devices with their start and end apart: 4 -> 0, of which waited for: 4 -> 0; matrix products, arithmetic and copies ran while one was open for 4% -> 0% of each run, Pallas kernels for 0% -> 0%
where the time goes in v1:
time: 68.7 us; the launch traced here: 68.4 us
  Pallas kernels  63.7 us (93%)
  local copies, waits for them, and re-layouts  4.71 us (7%)
    pallas_call x1, Pallas kernels, body(): pl.pallas_call(functools.partial(kernel, n, m, AC, NR), out_shape=jax.Sha...  63.7 us
    unnamed x3, local copies, waits for them, and re-layouts  4.71 us

profile of v1, /device:TPU:28, one launch (start us, length us, event | category | flops | bytes accessed | tf_op | source)
XLA Modules:
  0.0 68.4 jit_solution(12857478011757026186)
XLA Ops:
  0.0 1.4 %copy.12.ids = s32[128,8]{1,0:T(8,128)} copy(s32[128,8]{0,1:T(8,128)} %param.17) | data formatting | bytes 8192 | tf_op args[6]
  1.4 1.4 %copy.13.weights = f32[128,8]{1,0:T(8,128)} copy(f32[128,8]{0,1:T(8,128)} %param.18) | data formatting | bytes 8192 | tf_op args[7]
  2.8 63.7 %shard_map.109 = f32[128,1024]{1,0:T(8,128)} custom-call(f32[128,1024]{1,0:T(8,128)} %hidden.1, bf16[128,1024]{1,0:T(8,128)(2,1)} %queries.1, bf16[128,256]{1,0:T(8,128)(2,1)} %keys.1, bf16[128,256]{1,0:T(8,128)(2,1)} %values.1, bf16[4096,1024]{1,0:T(8,128)(2,1)} %out_proj.1, f32[1,1024]{1,0:T(1,128)} %bitcast.1, s32[128,8]{1,0:T(8,128)} %copy.12.ids, ...), custom_call_target="tpu_custom_call" | custom-call | flops 4000000000 | bytes 20000000 | tf_op jit(solution)/shard_map/pallas_call | solution.py:383
  66.5 1.9 %copy.15 = f32[128,1024]{1,0:T(8,128)} copy(f32[128,1024]{1,0:T(8,128)} %shard_map.109) | data formatting | bytes 1048576

commit v2 on v1

--- a/solution.py
+++ b/solution.py
@@ -29,8 +29,8 @@
     n, m, AC, NR,
     hidden, queries, keys, values, out_proj, gain, ids, weights, w_gate, w_up, w_down,
     out,
-    q_v, kv, wo, wg, wu, wd, hid,
-    m_s, acc_s, att, xe, outb, arr, selw, pdown, pin, mine, xs, xin, eo, ret,
+    q_v, kv, q_t, wo, wg, wu, wd, hid,
+    m_s, l_s, acc_s, att, xe, outb, arr, selw, pdown, pin, mine, xs, xin, eo, ret,
     lsem, kv_s, kv_r, kvf_s, kvf_r, att_s, att_r, attf_s,
     d_s, d_r, g_s, g_r, gf_s, p_s, p_r, x_s, x_r, r_s, r_r,
 ):
@@ -63,6 +63,49 @@
             return carry
         lax.fori_loop(lo, hi, step, 0)
 
+    def kv_sent():
+        def step(o):
+            @pl.when(c + o < n)
+            def _():
+                remote(half(c, p), half(c, p), kv_s.at[o], kv_r.at[c], c, sib).wait_send()
+            @pl.when(c - o >= 0)
+            def _():
+                s = c - o
+                remote(half(s, p), half(s, p), kvf_s.at[s], kvf_r.at[s], c, sib).wait_send()
+        loop(1, n, step)
+
+    def att_sent():
+        for k in range(AC):
+            for o in range(1, chips):
+                t = other(o) * 2 + p
+                remote(piece(j, k), piece(j, k), att_s.at[t, k], att_r.at[j, k], c, t).wait_send()
+                remote(piece(t, k), piece(t, k), attf_s.at[t, k], att_r.at[t, k], c, sib).wait_send()
+            remote(piece(j, k), piece(j, k), att_s.at[sib, k], att_r.at[j, k], c, sib).wait_send()
+
+    def rows_sent():
+        def step(s):
+            @pl.when(s > 0)
+            def _():
+                remote(outb.at[s], arr.at[j, c], d_s.at[s], d_r.at[c], c, sib).wait_send()
+            for o in range(1, chips):
+                t = other(o) * 2 + p
+                remote(arr.at[j, s], arr.at[j, s], g_s.at[t, s], g_r.at[j, s], c, t).wait_send()
+                remote(arr.at[t, s], arr.at[t, s], gf_s.at[t, s], g_r.at[t, s], c, sib).wait_send()
+            remote(arr.at[j, s], arr.at[j, s], g_s.at[sib, s], g_r.at[j, s], c, sib).wait_send()
+        loop(0, n, step)
+
+    def rest_sent():
+        for r in range(NR):
+            for o in range(chips):
+                pair(r, other(o)).wait_send()
+            for o in range(1, chips):
+                cross(r, o).wait_send()
+        def step(s):
+            @pl.when(s != c)
+            def _():
+                remote(eo.at[s], ret.at[c], r_s.at[s], r_r.at[c], s, j).wait_send()
+        loop(0, n, step)
+
     local = [
         pltpu.make_async_copy(keys.at[:, head_lanes], kv.at[c, :, pl.ds(0, HD)], lsem.at[0]),
         pltpu.make_async_copy(values.at[:, head_lanes], kv.at[c, :, pl.ds(HD, HD)], lsem.at[1]),
@@ -83,9 +126,6 @@
         pl.semaphore_signal(barrier, inc=1, device_id=(c, lax.rem(j + o, m)), device_id_type=pl.DeviceIdType.MESH)
     for copy in local[3:]:
         copy.start()
-    ones = jnp.ones((T, HD), BF)
-    for s in range(n):
-        kv[s, :, 2 * HD:] = ones
     local[0].wait()
     local[1].wait()
     pl.semaphore_wait(barrier, n - 1 + m - 1)
@@ -100,66 +140,81 @@
             remote(half(c, p), half(c, p), kv_s.at[o], kv_r.at[c], d, j).start()
     loop(1, n, kv_send)
 
-    col = lax.broadcasted_iota(jnp.int32, (T, C), 1)
-    expert_col = lax.div(col, SLOT)
-    slot_col = lax.rem(col, SLOT)
-    hit = jnp.zeros((T, C), F32)
-    weight = jnp.zeros((T, C), F32)
-    for k in range(ids.shape[1]):
-        same = ids[:, k : k + 1] == expert_col
+    slot_row = lax.broadcasted_iota(jnp.int32, (C, T), 0)
+    expert_row = lax.div(slot_row, SLOT)
+    place = lax.rem(slot_row, SLOT).astype(F32)
+    hit = jnp.zeros((C, T), F32)
+    weight = jnp.zeros((C, T), F32)
+    for k in range(ids.shape[0]):
+        same = ids[k : k + 1, :] == expert_row
         hit = hit + jnp.where(same, 1.0, 0.0)
-        weight = weight + jnp.where(same, weights[:, k : k + 1], 0.0)
+        weight = weight + jnp.where(same, weights[k : k + 1, :], 0.0)
     row_t = lax.broadcasted_iota(jnp.int32, (T, T), 0)
     col_t = lax.broadcasted_iota(jnp.int32, (T, T), 1)
-    earlier = jnp.where(col_t < row_t, 1.0, 0.0).astype(BF)
-    before = dot(earlier, hit.astype(BF))
-    chosen = jnp.where((before == slot_col.astype(F32)) & (hit > 0.5), 1.0, 0.0)
-    weight = weight * chosen
+    earlier = jnp.where(row_t < col_t, 1.0, 0.0).astype(BF)
+    before = dot(hit.astype(BF), earlier)
+    chosen = jnp.where((before == place) & (hit > 0.5), 1.0, 0.0)
+    weight = (weight * chosen).T
     w_hi = weight.astype(BF)
     selw[0] = w_hi
     selw[1] = (weight - w_hi.astype(F32)).astype(BF)
-    sel = chosen.T.astype(BF)
+    sel = chosen.astype(BF)
 
     factor = math.log2(math.e) / math.sqrt(HD)
-    causal = col_t <= row_t
+    W = min(256, LH * T)
+    causal = jnp.concatenate([row_t <= col_t] * (W // T), axis=1)
     local[2].wait()
-
-    def block(s, first):
-        k_blk = kv[s, :, :HD]
-        v_blk = kv[s, :, HD:]
-        for h in range(LH):
-            q_h = q_v[:, h * HD : (h + 1) * HD]
-            sc = lax.dot_general(q_h, k_blk, (((1,), (1,)), ((), ())), preferred_element_type=F32)
+    for h in range(LH):
+        q_t[:, h * T : (h + 1) * T] = q_v[:, h * HD : (h + 1) * HD].T
+
+    def block(k_blk, v_blk, first):
+        v_t = v_blk.T
+        for w in range(LH * T // W):
+            at = slice(w * W, (w + 1) * W)
+            sc = dot(k_blk, q_t[:, at])
             if first:
                 sc = jnp.where(causal, sc, masked_score)
-                top = jnp.broadcast_to(jnp.max(sc, axis=1, keepdims=True), (T, HD))
+                top = jnp.max(sc, axis=0, keepdims=True)
                 pr = jnp.where(causal, jnp.exp2((sc - top) * factor), 0.0)
-                acc_s[h] = dot(pr.astype(BF), v_blk)
+                l_s[:, at] = jnp.sum(pr, axis=0, keepdims=True)
+                acc_s[:, at] = dot(v_t, pr.astype(BF))
             else:
-                old = m_s[h]
-                top = jnp.maximum(old, jnp.max(sc, axis=1, keepdims=True))
+                old = m_s[:, at]
+                top = jnp.maximum(old, jnp.max(sc, axis=0, keepdims=True))
                 pr = jnp.exp2((sc - top) * factor)
                 keep = jnp.exp2((old - top) * factor)
-                acc_s[h] = acc_s[h] * jnp.concatenate([keep, keep], axis=1) + dot(pr.astype(BF), v_blk)
-            m_s[h] = top
-
-    block(c, True)
-
-    def kv_step(o):
-        s = c - o
-        @pl.when(s >= 0)
+                l_s[:, at] = l_s[:, at] * keep + jnp.sum(pr, axis=0, keepdims=True)
+                acc_s[:, at] = acc_s[:, at] * keep + dot(v_t, pr.astype(BF))
+            m_s[:, at] = top
+
+    block(kv[c, :, :HD], kv[c, :, HD:], True)
+
+    def kv_step(i):
+        for o in (2 * i - 1, 2 * i):
+            s = c - o
+            @pl.when(s >= 0)
+            def _():
+                remote(half(s, p), half(s, p), kv_s.at[0], kv_r.at[s], c, sib).wait_recv()
+                remote(half(s, p), half(s, p), kvf_s.at[s], kvf_r.at[s], c, sib).start()
+        hi = c - (2 * i - 3)
+        lo = hi - 1
+        def arrived(s):
+            remote(half(s, 1 - p), half(s, 1 - p), kvf_s.at[s], kvf_r.at[s], c, sib).wait_recv()
+        @pl.when((i > 1) & (lo >= 0))
         def _():
-            remote(half(s, p), half(s, p), kv_s.at[o], kv_r.at[s], c, sib).wait_recv()
-            remote(half(s, p), half(s, p), kvf_s.at[s], kvf_r.at[s], c, sib).start()
-        prev = s + 1
-        @pl.when((prev >= 0) & (o > 1))
+            arrived(hi)
+            arrived(lo)
+            both = kv[pl.ds(lo, 2)].reshape(2 * T, 2 * HD)
+            block(both[:, :HD], both[:, HD:], False)
+        @pl.when((i > 1) & (lo == -1))
         def _():
-            remote(half(prev, 1 - p), half(prev, 1 - p), kvf_s.at[prev], kvf_r.at[prev], c, sib).wait_recv()
-            block(prev, False)
-    loop(1, n + 1, kv_step)
+            arrived(hi)
+            block(kv[hi, :, :HD], kv[hi, :, HD:], False)
+    loop(1, n // 2 + 2, kv_step)
 
     for h in range(LH):
-        att[j, :, h * HD : (h + 1) * HD] = (acc_s[h, :, :HD] / acc_s[h, :, HD:]).astype(BF)
+        at = slice(h * T, (h + 1) * T)
+        att[j, :, h * HD : (h + 1) * HD] = (acc_s[:, at] / l_s[:, at]).T.astype(BF)
     FC = F // AC
 
     def piece(jj, k):
@@ -332,38 +387,10 @@
     back = ret[...].reshape(C, F)
     out[...] += dot(selw[0], back) + dot(selw[1], back)
 
-    def kv_done(o):
-        @pl.when(c + o < n)
-        def _():
-            remote(half(c, p), half(c, p), kv_s.at[o], kv_r.at[c], c, sib).wait_send()
-        @pl.when(c - o >= 0)
-        def _():
-            s = c - o
-            remote(half(s, p), half(s, p), kvf_s.at[s], kvf_r.at[s], c, sib).wait_send()
-        remote(outb.at[o], arr.at[j, c], d_s.at[o], d_r.at[c], c, sib).wait_send()
-    loop(1, n, kv_done)
-
-    def rest_done(s):
-        for o in range(1, chips):
-            t = other(o) * 2 + p
-            remote(arr.at[j, s], arr.at[j, s], g_s.at[t, s], g_r.at[j, s], c, t).wait_send()
-            remote(arr.at[t, s], arr.at[t, s], gf_s.at[t, s], g_r.at[t, s], c, sib).wait_send()
-        remote(arr.at[j, s], arr.at[j, s], g_s.at[sib, s], g_r.at[j, s], c, sib).wait_send()
-        @pl.when(s != c)
-        def _():
-            remote(eo.at[s], ret.at[c], r_s.at[s], r_r.at[c], s, j).wait_send()
-    loop(0, n, rest_done)
-    for k in range(AC):
-        for o in range(1, chips):
-            t = other(o) * 2 + p
-            remote(piece(j, k), piece(j, k), att_s.at[t, k], att_r.at[j, k], c, t).wait_send()
-            remote(piece(t, k), piece(t, k), attf_s.at[t, k], att_r.at[t, k], c, sib).wait_send()
-        remote(piece(j, k), piece(j, k), att_s.at[sib, k], att_r.at[j, k], c, sib).wait_send()
-    for r in range(NR):
-        for o in range(chips):
-            pair(r, other(o)).wait_send()
-        for o in range(1, chips):
-            cross(r, o).wait_send()
+    kv_sent()
+    att_sent()
+    rows_sent()
+    rest_sent()
 
 
 def body(hidden, queries, keys, values, out_proj, gain, ids, weights, w_gate, w_up, w_down):
@@ -387,14 +414,16 @@
         out_specs=vm,
         scratch_shapes=[
             V((T, F), BF),
-            V((n, T, 3 * HD), BF),
+            V((n, T, 2 * HD), BF),
+            V((HD, LH * T), BF),
             V(out_proj.shape, BF),
             V(w_gate.shape[1:], BF),
             V(w_up.shape[1:], BF),
             V(w_down.shape[1:], BF),
             V((T, F), F32),
-            V((LH, T, HD), F32),
-            V((LH, T, 2 * HD), F32),
+            V((1, LH * T), F32),
+            V((1, LH * T), F32),
+            V((HD, LH * T), F32),
             V((m, T, F), BF),
             V((T, F + EXTRA), BF),
             V((n, SLOT, F + EXTRA), BF),
@@ -421,7 +450,7 @@
         ),
         cost_estimate=pl.CostEstimate(flops=4 * 10**9, bytes_accessed=2 * 10**7, transcendentals=10**6),
     )(
-        hidden, queries, keys, values, out_proj, gain.reshape(1, F), ids, weights,
+        hidden, queries, keys, values, out_proj, gain.reshape(1, F), ids.T, weights.T,
         w_gate, w_up, w_down,
     )
 

time: 68.7 us -> 59 us (0.86)
  Pallas kernels: 63.7 us -> 56.9 us
  local copies, waits for them, and re-layouts: 4.71 us -> 1.89 us
    pallas_call x1, Pallas kernels: 63.7 us -> 56.9 us  [body(): pl.pallas_call(functools.partial(kernel, n, m, AC, NR), out_shape=jax.Sha...]
    unnamed x3 -> x1, local copies, waits for them, and re-layouts: 4.71 us -> 1.89 us
where the time goes in v2:
time: 59 us; the launch traced here: 58.8 us
  Pallas kernels  56.9 us (96%)
  local copies, waits for them, and re-layouts  1.89 us (3%)
    pallas_call x1, Pallas kernels, body(): pl.pallas_call(functools.partial(kernel, n, m, AC, NR), out_shape=jax.Sha...  56.9 us
    unnamed x1, local copies, waits for them, and re-layouts  1.89 us

profile of v2, /device:TPU:28, one launch (start us, length us, event | category | flops | bytes accessed | tf_op | source)
XLA Modules:
  0.0 58.8 jit_solution(8222021192180757977)
XLA Ops:
  0.0 56.9 %shard_map.109 = f32[128,1024]{1,0:T(8,128)} custom-call(f32[128,1024]{1,0:T(8,128)} %hidden.1, bf16[128,1024]{1,0:T(8,128)(2,1)} %queries.1, bf16[128,256]{1,0:T(8,128)(2,1)} %keys.1, bf16[128,256]{1,0:T(8,128)(2,1)} %values.1, bf16[4096,1024]{1,0:T(8,128)(2,1)} %out_proj.1, f32[1,1024]{1,0:T(1,128)} %bitcast.3, s32[8,128]{1,0:T(8,128)} %bitcast.4, ...), custom_call_target="tpu_custom_call" | custom-call | flops 4000000000 | bytes 20000000 | tf_op jit(solution)/shard_map/pallas_call | solution.py:410
  56.9 1.9 %copy.13 = f32[128,1024]{1,0:T(8,128)} copy(f32[128,1024]{1,0:T(8,128)} %shard_map.109) | data formatting | bytes 1048576

commit v3 on v2

--- a/solution.py
+++ b/solution.py
@@ -12,6 +12,7 @@
 HEADS = 32
 KV_HEADS = 2
 HD = 128
+CAP = 12
 SLOT = 16
 EXTRA = 128
 
@@ -26,7 +27,7 @@
 
 
 def kernel(
-    n, m, AC, NR,
+    n, m, AC, NR, G, LAGS,
     hidden, queries, keys, values, out_proj, gain, ids, weights, w_gate, w_up, w_down,
     out,
     q_v, kv, q_t, wo, wg, wu, wd, hid,
@@ -40,6 +41,10 @@
     C = n * SLOT
     U = w_gate.shape[2]
     chips = m // 2
+    NG = n // G
+    FP = arr.shape[3] - EXTRA
+    FQ = F - FP
+    groups = FP // FQ if FQ else 0
     c = lax.axis_index("ctx")
     j = lax.axis_index("et")
     p = lax.rem(j, 2)
@@ -84,15 +89,16 @@
 
     def rows_sent():
         def step(s):
-            @pl.when(s > 0)
-            def _():
-                remote(outb.at[s], arr.at[j, c], d_s.at[s], d_r.at[c], c, sib).wait_send()
+            remote(outb.at[s], arr.at[j, c], d_s.at[s], d_r.at[c], c, sib).wait_send()
+        loop(1, n, step)
+
+        def step_group(i):
             for o in range(1, chips):
                 t = other(o) * 2 + p
-                remote(arr.at[j, s], arr.at[j, s], g_s.at[t, s], g_r.at[j, s], c, t).wait_send()
-                remote(arr.at[t, s], arr.at[t, s], gf_s.at[t, s], g_r.at[t, s], c, sib).wait_send()
-            remote(arr.at[j, s], arr.at[j, s], g_s.at[sib, s], g_r.at[j, s], c, sib).wait_send()
-        loop(0, n, step)
+                remote(rows(j, i), rows(j, i), g_s.at[t, i], g_r.at[j, i], c, t).wait_send()
+                remote(rows(t, i), rows(t, i), gf_s.at[t, i], g_r.at[t, i], c, sib).wait_send()
+            remote(rows(j, i), rows(j, i), g_s.at[sib, i], g_r.at[j, i], c, sib).wait_send()
+        loop(0, NG, step_group)
 
     def rest_sent():
         for r in range(NR):
@@ -124,8 +130,6 @@
         pl.semaphore_signal(barrier, inc=1, device_id=(lax.rem(c + o, n), j), device_id_type=pl.DeviceIdType.MESH)
     for o in range(1, m):
         pl.semaphore_signal(barrier, inc=1, device_id=(c, lax.rem(j + o, m)), device_id_type=pl.DeviceIdType.MESH)
-    for copy in local[3:]:
-        copy.start()
     local[0].wait()
     local[1].wait()
     pl.semaphore_wait(barrier, n - 1 + m - 1)
@@ -139,6 +143,8 @@
         def _():
             remote(half(c, p), half(c, p), kv_s.at[o], kv_r.at[c], d, j).start()
     loop(1, n, kv_send)
+    for copy in local[3:5]:
+        copy.start()
 
     slot_row = lax.broadcasted_iota(jnp.int32, (C, T), 0)
     expert_row = lax.div(slot_row, SLOT)
@@ -154,11 +160,28 @@
     earlier = jnp.where(row_t < col_t, 1.0, 0.0).astype(BF)
     before = dot(hit.astype(BF), earlier)
     chosen = jnp.where((before == place) & (hit > 0.5), 1.0, 0.0)
-    weight = (weight * chosen).T
-    w_hi = weight.astype(BF)
-    selw[0] = w_hi
-    selw[1] = (weight - w_hi.astype(F32)).astype(BF)
     sel = chosen.astype(BF)
+    sel_tail = []
+
+    def keep_weights(i, table):
+        w = (weight * table).T
+        w_hi = w.astype(BF)
+        selw[2 * i] = w_hi
+        selw[2 * i + 1] = (w - w_hi.astype(F32)).astype(BF)
+
+    keep_weights(0, chosen)
+    for g in range(groups):
+        tail = jnp.where((place >= CAP) & (before == 3 * (place - CAP) + g) & (hit > 0.5), 1.0, 0.0)
+        sel_tail.append(tail.astype(BF))
+        keep_weights(1 + g, tail)
+    slot_a = lax.broadcasted_iota(jnp.int32, (C, C), 0)
+    slot_b = lax.broadcasted_iota(jnp.int32, (C, C), 1)
+
+    def unpack(row, tail, g):
+        at, to = lax.rem(row, SLOT), lax.rem(tail, SLOT)
+        same = lax.div(row, SLOT) == lax.div(tail, SLOT)
+        there = (to >= CAP) & (3 * (to - CAP) + g == at)
+        return jnp.where(same & there, 1.0, 0.0).astype(BF)
 
     factor = math.log2(math.e) / math.sqrt(HD)
     W = min(256, LH * T)
@@ -212,6 +235,8 @@
             block(kv[hi, :, :HD], kv[hi, :, HD:], False)
     loop(1, n // 2 + 2, kv_step)
 
+    for copy in local[5:8]:
+        copy.start()
     for h in range(LH):
         at = slice(h * T, (h + 1) * T)
         att[j, :, h * HD : (h + 1) * HD] = (acc_s[:, at] / l_s[:, at]).T.astype(BF)
@@ -261,7 +286,13 @@
     xe[:, F:] = jnp.where(
         lane == 0, part0, jnp.where(lane == 1, part1, jnp.where(lane == 2, part2, 0.0))
     ).astype(BF)
-    outb[...] = dot(sel, xe[...]).astype(BF).reshape(n, SLOT, F + EXTRA)
+    outb[:, :, FP:] = dot(sel, xe[:, F:]).astype(BF).reshape(n, SLOT, EXTRA)
+    if groups == 0:
+        outb[:, :, :FP] = dot(sel, xe[:, :F]).astype(BF).reshape(n, SLOT, FP)
+    for g in range(groups):
+        at = slice(g * FQ, (g + 1) * FQ)
+        got = dot(sel, xe[:, at]) + dot(sel_tail[g], xe[:, FP:F])
+        outb[:, :, at] = got.astype(BF).reshape(n, SLOT, FQ)
 
     def d_send(o):
         d = lax.rem(c + o, n)
@@ -269,31 +300,51 @@
     loop(1, n, d_send)
     arr[j, c] = outb[c]
 
-    def spread(s):
+    LAG = min(LAGS, NG - 1)
+    own_group = lax.div(c, G)
+
+    def rows(t, i):
+        return arr.at[t, pl.ds(i * G, G)]
+
+    def spread(i):
         for o in range(1, chips):
             t = other(o) * 2 + p
-            remote(arr.at[j, s], arr.at[j, s], g_s.at[t, s], g_r.at[j, s], c, t).start()
-        remote(arr.at[j, s], arr.at[j, s], g_s.at[sib, s], g_r.at[j, s], c, sib).start()
+            remote(rows(j, i), rows(j, i), g_s.at[t, i], g_r.at[j, i], c, t).start()
+        remote(rows(j, i), rows(j, i), g_s.at[sib, i], g_r.at[j, i], c, sib).start()
+
+    def g_step(o):
+        i = lax.rem(own_group + NG - o, NG)
+        for o in range(1, chips):
+            t = other(o) * 2 + p
+            remote(rows(t, i), rows(t, i), g_s.at[t, i], g_r.at[t, i], c, sib).wait_recv()
+            remote(rows(t, i), rows(t, i), gf_s.at[t, i], g_r.at[t, i], c, sib).start()
 
     def d_step(o):
-        s = lax.rem(c + n - o, n)
-        @pl.when(o > 0)
+        i = lax.rem(own_group + NG - o, NG)
+        for k in range(G):
+            s = i * G + k
+            @pl.when(s != c)
+            def _():
+                remote(outb.at[s], arr.at[j, s], d_s.at[0], d_r.at[s], c, sib).wait_recv()
+        spread(i)
+        @pl.when(o >= LAG)
         def _():
-            remote(outb.at[s], arr.at[j, s], d_s.at[o], d_r.at[s], c, sib).wait_recv()
-        spread(s)
-    loop(0, n, d_step)
+            g_step(o - LAG)
+    loop(0, NG, d_step)
 
     for i in range(5, 8):
         local[i].wait()
 
-    def rows_of(t):
-        return arr[t].reshape(C, F + EXTRA)
-
     def pre(t):
-        x = rows_of(t)
-        at = pl.ds(pl.multiple_of(t * F, F), F)
-        sq = jnp.sum(x[:, F:].astype(F32), axis=1, keepdims=True)
-        return dot(x[:, :F], wg[at, :]), dot(x[:, :F], wu[at, :]), sq
+        x = arr[t].reshape(C, FP + EXTRA)
+        at = pl.ds(pl.multiple_of(t * F, F), FP)
+        sq = jnp.sum(x[:, FP:].astype(F32), axis=1, keepdims=True)
+        gate, up = dot(x[:, :FP], wg[at, :]), dot(x[:, :FP], wu[at, :])
+        if groups:
+            tail = sum(dot(unpack(slot_a, slot_b, g), x[:, g * FQ : (g + 1) * FQ]) for g in range(groups)).astype(BF)
+            at = pl.ds(pl.multiple_of(t * F + FP, FQ), FQ)
+            gate, up = gate + dot(tail, wg[at, :]), up + dot(tail, wu[at, :])
+        return gate, up, sq
 
     gate, up, sq = pre(j)
 
@@ -301,18 +352,12 @@
         g1, u1, s1 = pre(t)
         return gate + g1, up + u1, sq + s1
 
-    for o in range(1, chips):
-        t = other(o) * 2 + p
-        def g_step(i):
-            s = lax.rem(c + n - i, n)
-            remote(arr.at[t, s], arr.at[t, s], g_s.at[t, s], g_r.at[t, s], c, sib).wait_recv()
-            remote(arr.at[t, s], arr.at[t, s], gf_s.at[t, s], g_r.at[t, s], c, sib).start()
-        loop(0, n, g_step)
+    loop(NG - LAG, NG, g_step)
 
     def g_wait(t):
-        def step(s):
-            remote(arr.at[t, s], arr.at[t, s], g_s.at[t, s], g_r.at[t, s], c, sib).wait_recv()
-        loop(0, n, step)
+        def step(i):
+            remote(rows(t, i), rows(t, i), g_s.at[t, i], g_r.at[t, i], c, sib).wait_recv()
+        loop(0, NG, step)
 
     g_wait(sib)
     gate, up, sq = add(sib, gate, up, sq)
@@ -322,7 +367,8 @@
         t = other(o) * 2 + 1 - p
         g_wait(t)
         gate, up, sq = add(t, gate, up, sq)
-    scale = lax.rsqrt(sq / D + epsilon)
+    used = lax.rem(lax.broadcasted_iota(jnp.int32, (C, 1), 0), SLOT) < CAP
+    scale = jnp.where(used, lax.rsqrt(sq / D + epsilon), 0.0)
     gate = gate * scale
     up = up * scale
     act = (gate / (1.0 + jnp.exp(-gate)) * up).astype(BF)
@@ -330,8 +376,15 @@
     CR = C // NR
     NC = n // NR
 
+    moved = [dot(unpack(slot_b, slot_a, g), act).astype(BF) for g in range(groups)]
+
     def down(t, r):
-        return dot(act[r * CR : (r + 1) * CR], wd[:, pl.ds(pl.multiple_of(t * F, F), F)])
+        rr = slice(r * CR, (r + 1) * CR)
+        got = dot(act[rr], wd[:, pl.ds(pl.multiple_of(t * F, F), FP)])
+        if groups:
+            last = wd[:, pl.ds(pl.multiple_of(t * F + FP, FQ), FQ)]
+            got = got + jnp.concatenate([dot(x[rr], last) for x in moved], axis=1)
+        return got
 
     def at_rows(r):
         return pl.ds(r * CR, CR)
@@ -368,7 +421,7 @@
             q = other(o)
             remote(xin.at[q, at_rows(r)], xin.at[q, at_rows(r)], x_s.at[q, r], x_r.at[q, r], c, sib).wait_recv()
             total = total + xin[q, rr].astype(F32)
-        eo[r * NC : (r + 1) * NC] = total.astype(BF).reshape(NC, SLOT, F)
+        eo[r * NC : (r + 1) * NC] = total.astype(BF).reshape(NC, SLOT, FP)
 
         def r_send(s):
             @pl.when(s != c)
@@ -384,8 +437,11 @@
         def _():
             remote(eo.at[s], ret.at[s], r_s.at[s], r_r.at[s], s, j).wait_recv()
     loop(0, n, r_wait)
-    back = ret[...].reshape(C, F)
-    out[...] += dot(selw[0], back) + dot(selw[1], back)
+    back = ret[...].reshape(C, FP)
+    out[:, :FP] += dot(selw[0], back) + dot(selw[1], back)
+    for g in range(groups):
+        piece_g = back[:, g * FQ : (g + 1) * FQ]
+        out[:, FP:] += dot(selw[2 + 2 * g], piece_g) + dot(selw[3 + 2 * g], piece_g)
 
     kv_sent()
     att_sent()
@@ -403,12 +459,15 @@
     chips = m // 2
     AC = 4 if F % 512 == 0 else 2
     NR = 2
+    G = 2
+    LAGS = 7
+    FP = F * CAP // SLOT if F % (128 * SLOT // (SLOT - CAP)) == 0 else F
     DMA = pltpu.SemaphoreType.DMA
     V = pltpu.VMEM
     any_ = pl.BlockSpec(memory_space=pl.ANY)
     vm = pl.BlockSpec(memory_space=pltpu.VMEM)
     return pl.pallas_call(
-        functools.partial(kernel, n, m, AC, NR),
+        functools.partial(kernel, n, m, AC, NR, G, LAGS),
         out_shape=jax.ShapeDtypeStruct((T, F), F32),
         in_specs=[any_, any_, any_, any_, any_, vm, vm, vm, any_, any_, any_],
         out_specs=vm,
@@ -426,21 +485,21 @@
             V((HD, LH * T), F32),
             V((m, T, F), BF),
             V((T, F + EXTRA), BF),
-            V((n, SLOT, F + EXTRA), BF),
-            V((m, n, SLOT, F + EXTRA), BF),
-            V((2, T, C), BF),
-            V((chips, C, F), BF),
-            V((chips, C, F), BF),
-            V((C, F), F32),
-            V((chips, C, F), BF),
-            V((chips, C, F), BF),
-            V((n, SLOT, F), BF),
-            V((n, SLOT, F), BF),
+            V((n, SLOT, FP + EXTRA), BF),
+            V((m, n, SLOT, FP + EXTRA), BF),
+            V((8, T, C), BF),
+            V((chips, C, FP), BF),
+            V((chips, C, FP), BF),
+            V((C, FP), F32),
+            V((chips, C, FP), BF),
+            V((chips, C, FP), BF),
+            V((n, SLOT, FP), BF),
+            V((n, SLOT, FP), BF),
             DMA((8,)),
             DMA((n,)), DMA((n,)), DMA((n,)), DMA((n,)),
             DMA((m, AC)), DMA((m, AC)), DMA((m, AC)),
             DMA((n,)), DMA((n,)),
-            DMA((m, n)), DMA((m, n)), DMA((m, n)),
+            DMA((m, n // G)), DMA((m, n // G)), DMA((m, n // G)),
             DMA((chips, NR)), DMA((chips, NR)),
             DMA((chips, NR)), DMA((chips, NR)),
             DMA((n,)), DMA((n,)),

time: 59 us -> 55.1 us (0.934)
  Pallas kernels: 56.9 us -> 52.4 us
    pallas_call x1, Pallas kernels: 56.9 us -> 52.4 us  [body(): pl.pallas_call(functools.partial(kernel, n, m, AC, NR, G, LAGS), out_shap...]
where the time goes in v3:
time: 55.1 us; the launch traced here: 54.3 us
  Pallas kernels  52.4 us (95%)
  local copies, waits for them, and re-layouts  1.89 us (3%)
    pallas_call x1, Pallas kernels, body(): pl.pallas_call(functools.partial(kernel, n, m, AC, NR, G, LAGS), out_shap...  52.4 us
    unnamed x1, local copies, waits for them, and re-layouts  1.89 us

profile of v3, /device:TPU:28, one launch (start us, length us, event | category | flops | bytes accessed | tf_op | source)
XLA Modules:
  0.0 54.3 jit_solution(11318099070121169244)
XLA Ops:
  0.0 52.4 %shard_map.109 = f32[128,1024]{1,0:T(8,128)} custom-call(f32[128,1024]{1,0:T(8,128)} %hidden.1, bf16[128,1024]{1,0:T(8,128)(2,1)} %queries.1, bf16[128,256]{1,0:T(8,128)(2,1)} %keys.1, bf16[128,256]{1,0:T(8,128)(2,1)} %values.1, bf16[4096,1024]{1,0:T(8,128)(2,1)} %out_proj.1, f32[1,1024]{1,0:T(1,128)} %bitcast.3, s32[8,128]{1,0:T(8,128)} %bitcast.4, ...), custom_call_target="tpu_custom_call" | custom-call | flops 4000000000 | bytes 20000000 | tf_op jit(solution)/shard_map/pallas_call | solution.py:469
  52.4 1.9 %copy.13 = f32[128,1024]{1,0:T(8,128)} copy(f32[128,1024]{1,0:T(8,128)} %shard_map.109) | data formatting | bytes 1048576

commit v4 on v3

--- a/solution.py
+++ b/solution.py
@@ -397,7 +397,7 @@
         return remote(xs.at[q, at_rows(r)], xin.at[chip, at_rows(r)], x_s.at[q, r], x_r.at[chip, r], c, q * 2 + p)
 
     for r in range(NR):
-        for o in list(range(1, chips)) + [0]:
+        for o in range(1, chips):
             q = other(o)
             pdown[q, r * CR : (r + 1) * CR] = down(q * 2 + 1 - p, r).astype(BF)
             pair(r, q).start()
@@ -409,6 +409,11 @@
             pair(r, q).wait_recv()
             xs[q, rr] = (part + pin[q, rr].astype(F32)).astype(BF)
             cross(r, o).start()
+    for r in range(NR):
+        for o in [0]:
+            q = other(o)
+            pdown[q, r * CR : (r + 1) * CR] = down(q * 2 + 1 - p, r).astype(BF)
+            pair(r, q).start()
     for r in range(NR):
         rr = slice(r * CR, (r + 1) * CR)
         mine[rr] = down(chip * 2 + p, r).astype(BF).astype(F32)

time: 55.1 us -> 55 us (level)
  no operation moved by 1% of the time
where the time goes in v4:
time: 55 us; the launch traced here: 54.3 us
  Pallas kernels  52.4 us (95%)
  local copies, waits for them, and re-layouts  1.89 us (3%)
    pallas_call x1, Pallas kernels, body(): pl.pallas_call(functools.partial(kernel, n, m, AC, NR, G, LAGS), out_shap...  52.4 us
    unnamed x1, local copies, waits for them, and re-layouts  1.89 us

profile of v4, /device:TPU:28, one launch (start us, length us, event | category | flops | bytes accessed | tf_op | source)
XLA Modules:
  0.0 54.3 jit_solution(9144233442640196161)
XLA Ops:
  0.0 52.4 %shard_map.109 = f32[128,1024]{1,0:T(8,128)} custom-call(f32[128,1024]{1,0:T(8,128)} %hidden.1, bf16[128,1024]{1,0:T(8,128)(2,1)} %queries.1, bf16[128,256]{1,0:T(8,128)(2,1)} %keys.1, bf16[128,256]{1,0:T(8,128)(2,1)} %values.1, bf16[4096,1024]{1,0:T(8,128)(2,1)} %out_proj.1, f32[1,1024]{1,0:T(1,128)} %bitcast.3, s32[8,128]{1,0:T(8,128)} %bitcast.4, ...), custom_call_target="tpu_custom_call" | custom-call | flops 4000000000 | bytes 20000000 | tf_op jit(solution)/shard_map/pallas_call | solution.py:474
  52.4 1.9 %copy.13 = f32[128,1024]{1,0:T(8,128)} copy(f32[128,1024]{1,0:T(8,128)} %shard_map.109) | data formatting | bytes 1048576
